TPU v7x, 128 devices: a whole 4x4x4 slice. The times are simulated.
128 devices in a mesh: lat: 8 (over x, z_hi), lon: 16 (over y, z_lo, core).
Axes of the slice: x: 4, y: 4, z: 4 (z_hi: 2, z_lo: 2; z = z_hi * 2 + z_lo), core: 2. Of those that a mesh axis runs over, the one named last changes fastest.
Arguments:
- latents: bfloat16 [2, 96, 1152, 512], P(None, 'lat', 'lon'), may hold values from -6 to 6
- attend_gain: float32 [512], replicated, may hold values from 0.1 to 1.9
- packed_heads: bfloat16 [512, 1536], P('lon'), may hold values from -4 to 4
- heads_back: bfloat16 [512, 512], P('lon'), may hold values from -0.25 to 0.25
- dense_gain: float32 [512], replicated, may hold values from 0.1 to 1.9
- expand_weight: bfloat16 [512, 2048], P('lon'), may hold values from -0.25 to 0.25
- shrink_weight: bfloat16 [2048, 512], P('lon'), may hold values from -0.125 to 0.125
- merge_gain: float32 [2048], replicated, may hold values from 0.1 to 1.9
- merge_weight: bfloat16 [2048, 1024], P('lon'), may hold values from -0.125 to 0.125
- coarse_gain: float32 [1024], replicated, may hold values from 0.1 to 1.9
- coarse_heads: bfloat16 [1024, 3072], P('lon'), may hold values from -4 to 4
- coarse_back: bfloat16 [1024, 1024], P('lon'), may hold values from -0.1875 to 0.1875
- coarse_scale: float32 [1024], replicated, may hold values from 0.1 to 1.9
- coarse_expand: bfloat16 [1024, 4096], P('lon'), may hold values from -0.1875 to 0.1875
- coarse_shrink: bfloat16 [4096, 1024], P('lon'), may hold values from -0.09375 to 0.09375
Outputs:
- coarse_latents: bfloat16 [2, 48, 576, 1024], P(None, 'lat', 'lon')
All inputs are finite; a program needn't handle non-finite values.
Results may differ from a plain program's by a relative error of at most 0.034.
Values may be sent and summed in bfloat16 or wider, within the bound.
No kernel may reach another device: no remote copies, remote signals or barrier semaphores. Data moves between devices by JAX's collectives and lax.ppermute only.
A program may use at most 192 MiB of HBM per device.

v0:
```python
import jax
import jax.numpy as jnp
from jax import lax
from jax.sharding import PartitionSpec as P

HEAD = 64
WIN_LEV = 2
WIN_LAT = 6
WIN_LON = 12


EPS = 1e-05
SCALE = 0.125


def passed_along(value, axis, steps):
    count = lax.axis_size(axis)
    pairs = [(source, (source + steps) % count) for source in range(count)]
    return lax.ppermute(value, axis, pairs)


def layer_norm(values, gain):
    values = values.astype(jnp.float32)
    center = values - jnp.mean(values, -1, keepdims=True)
    spread = jnp.mean(center * center, -1, keepdims=True)
    return center * lax.rsqrt(spread + EPS) * gain


def window_split(grid):
    levels, rows, cols, width = grid.shape
    parts = grid.reshape(
        levels // WIN_LEV, WIN_LEV, rows // WIN_LAT, WIN_LAT, cols // WIN_LON, WIN_LON, width
    )
    parts = parts.transpose(0, 2, 4, 1, 3, 5, 6)
    return parts.reshape(-1, WIN_LEV * WIN_LAT * WIN_LON, width)


def window_join(parts, levels, rows, cols):
    width = parts.shape[-1]
    grid = parts.reshape(
        levels // WIN_LEV, rows // WIN_LAT, cols // WIN_LON, WIN_LEV, WIN_LAT, WIN_LON, width
    )
    return grid.transpose(0, 3, 1, 4, 2, 5, 6).reshape(levels, rows, cols, width)


def project(values, shard):
    return jnp.dot(
        values, lax.all_gather(shard, "lon", axis=0, tiled=True), preferred_element_type=jnp.float32
    )


def roll_lat(grid, forward):
    cut = WIN_LAT // 2
    height = grid.shape[1]
    edge = grid[:, :cut] if forward else grid[:, height - cut :]
    moved = passed_along(edge, "lat", -1 if forward else 1)
    if forward:
        return jnp.concatenate([grid[:, cut:], moved], 1)
    return jnp.concatenate([moved, grid[:, : height - cut]], 1)


def roll_lon(grid, forward):
    cut = WIN_LON // 2
    breadth = grid.shape[2]
    edge = grid[:, :, :cut] if forward else grid[:, :, breadth - cut :]
    moved = passed_along(edge, "lon", -1 if forward else 1)
    if forward:
        return jnp.concatenate([grid[:, :, cut:], moved], 2)
    return jnp.concatenate([moved, grid[:, :, : breadth - cut]], 2)


def attend(parts, flags, gain, linear):
    groups, count, width = parts.shape
    heads = width // HEAD
    flat = parts.reshape(-1, width)
    normed = layer_norm(flat, gain).astype(jnp.bfloat16)
    qkv = linear(normed, 0).astype(jnp.bfloat16).reshape(groups, count, 3, heads, HEAD)
    scores = (
        jnp.einsum(
            "gqhe,gkhe->ghqk", qkv[:, :, 0], qkv[:, :, 1], preferred_element_type=jnp.float32
        )
        * SCALE
    )
    if flags is not None:
        same = flags[:, :, None] == flags[:, None, :]
        scores = jnp.where(same[:, None], scores, -1e30)
    top = jnp.max(scores, -1, keepdims=True)
    weights = jnp.exp(scores - top)
    probs = (weights / jnp.sum(weights, -1, keepdims=True)).astype(jnp.bfloat16)
    context = jnp.einsum(
        "ghqk,gkhe->gqhe", probs, qkv[:, :, 2], preferred_element_type=jnp.float32
    ).astype(jnp.bfloat16)
    return (flat.astype(jnp.float32) + linear(context.reshape(-1, width), 1)).astype(jnp.bfloat16)


def dense(flat, gain, linear):
    hidden = layer_norm(flat, gain).astype(jnp.bfloat16)
    expanded = jax.nn.gelu(linear(hidden, 2), approximate=False).astype(jnp.bfloat16)
    return (flat.astype(jnp.float32) + linear(expanded, 3)).astype(jnp.bfloat16)


def per_device(
    latents,
    attend_gain,
    packed_heads,
    heads_back,
    dense_gain,
    expand_weight,
    shrink_weight,
    merge_gain,
    merge_weight,
    coarse_gain,
    coarse_heads,
    coarse_back,
    coarse_scale,
    coarse_expand,
    coarse_shrink,
):
    levels, rows, cols, width = latents.shape
    lat_cut = WIN_LAT // 2
    coarse_shards = (coarse_heads, coarse_back, coarse_expand, coarse_shrink)

    def coarse_linear(values, index):
        return project(values, coarse_shards[index])

    fine_shards = (packed_heads, heads_back, expand_weight, shrink_weight)

    def fine_linear(values, index):
        return project(values, fine_shards[index])

    rolled = roll_lon(roll_lat(latents, True), True)
    total_rows = rows * lax.axis_size("lat")
    row_ids = lax.axis_index("lat") * rows + jnp.arange(rows, dtype=jnp.int32)
    row_flags = (row_ids >= total_rows - lat_cut).astype(jnp.int32)
    spread_flags = jnp.broadcast_to(row_flags[None, :, None, None], (levels, rows, cols, 1))
    token_flags = window_split(spread_flags)[:, :, 0]
    parts = window_split(rolled)
    mixed = attend(parts, token_flags, attend_gain, fine_linear)
    grid = window_join(mixed.reshape(parts.shape), levels, rows, cols)
    placed = roll_lon(roll_lat(grid, False), False)
    done = dense(placed.reshape(-1, width), dense_gain, fine_linear)
    first = done.reshape(levels, rows, cols, width)
    quads = first.reshape(levels, rows // 2, 2, cols // 2, 2, width).transpose(0, 1, 3, 4, 2, 5)
    quads = quads.reshape(-1, 4 * width)
    normed = layer_norm(quads, merge_gain).astype(jnp.bfloat16)
    merged = project(normed, merge_weight).astype(jnp.bfloat16)
    coarse = merged.reshape(levels, rows // 2, cols // 2, 2 * width)
    coarse_parts = window_split(coarse)
    coarse_mixed = attend(coarse_parts, None, coarse_gain, coarse_linear)
    finished = dense(coarse_mixed, coarse_scale, coarse_linear)
    return window_join(finished.reshape(coarse_parts.shape), levels, rows // 2, cols // 2)


def solution(mesh):
    in_specs = (
        P(None, "lat", "lon", None),
        P(),
        P("lon", None),
        P("lon", None),
        P(),
        P("lon", None),
        P("lon", None),
        P(),
        P("lon", None),
        P(),
        P("lon", None),
        P("lon", None),
        P(),
        P("lon", None),
        P("lon", None),
    )
    out_specs = P(None, "lat", "lon", None)
    return jax.shard_map(
        per_device, mesh=mesh, in_specs=in_specs, out_specs=out_specs, check_vma=False
    )
```

profile of v0, /device:TPU:1, one launch (start us, length us, event | category | flops | bytes accessed | tf_op | source)
XLA Modules:
  0.0 398.9 jit_solution(9688539368859098496)
XLA Ops:
  12.3 6.7 %collective-permute-start = (bf16[2,3,72,512]{3,2,1,0:T(8,128)(2,1)S(1)}, bf16[2,3,72,512]{3,2,1,0:T(8,128)(2,1)S(1)}, u32[]{:S(2)}, u32[]{:S(2)}) collective-permute-start(bf16[2,3,72,512]{3,2,1,0:T(8,128)(2,1)S(1)} %slice.43), channel_id=1, source_target_pairs={{0,112},{16,0},{32,16},{48,32},{64,48},{80,64},{96,80},{112,96},{1... | collective-permute-start | bytes 1327112 | tf_op jit(solution)/shard_map/ppermute | solution.py:19
  21.7 25.4 %all_gather.28 = bf16[512,512]{1,0:T(8,128)(2,1)} all-gather(bf16[32,512]{1,0:T(8,128)(2,1)} %param.18), channel_id=1, replica_groups=mesh['lat'=8,'lon'=16] {'lon'}, dimensions={0}, use_global_device_ids=true | all-gather | bytes 557056 | tf_op jit(solution)/shard_map/all_gather | solution.py:48
  47.9 5.0 %collective-permute-done.1 = bf16[2,12,6,512]{3,2,1,0:T(8,128)(2,1)S(1)} collective-permute-done((bf16[2,12,6,512]{3,2,1,0:T(8,128)(2,1)S(1)}, bf16[2,12,6,512]{3,2,1,0:T(8,128)(2,1)S(1)}, u32[]{:S(2)}, u32[]{:S(2)}) %collective-permute-start.1) | collective-permute-done | bytes 147488 | tf_op jit(solution)/shard_map/ppermute | solution.py:19
  74.3 6.6 %convolution_convert_fusion = bf16[1728,1536]{1,0:T(8,128)(2,1)} fusion(bf16[512,1536]{1,0:T(8,128)(2,1)} %all-gather.9.cloned.1.call-done, f32[1728,512]{1,0:T(8,128)S(1)} %reshape.215, f32[512]{0:T(512)} %param.16, f32[1728]{0:T(1024)S(1)} %rsqrt.53, f32[1728]{0:T(1024)S(1)} %div.55), kind=kOutput, calls=%fused_computation.26 | convolution fusion | flops 2724102144 | bytes 10436096 | tf_op jit(solution)/shard_map/dot_general | solution.py:47
  80.9 13.9 %reshape.209 = bf16[12,144,3,8,64]{4,3,2,1,0:T(8,128)(2,1)} reshape(bf16[1728,1536]{1,0:T(8,128)(2,1)} %convolution_convert_fusion) | data formatting | bytes 10616832 | tf_op jit(solution)/shard_map/reshape | solution.py:77
  94.9 6.4 %fusion.166 = (bf16[12,144,1,8,64]{4,3,2,1,0:T(8,128)(2,1)S(1)}, bf16[12,144,1,8,64]{4,3,2,1,0:T(8,128)(2,1)}, bf16[12,144,1,8,64]{4,3,2,1,0:T(8,128)(2,1)}) fusion(bf16[12,144,3,8,64]{4,3,2,1,0:T(8,128)(2,1)} %reshape.209), kind=kLoop, calls=%fused_computation.197 | loop fusion | bytes 10616832 | tf_op jit(solution)/shard_map/slice | solution.py:91
  101.3 6.2 %copy.121 = bf16[12,144,1,8,64]{1,4,3,0,2:T(8,128)(2,1)} copy(bf16[12,144,1,8,64]{4,3,2,1,0:T(8,128)(2,1)} %get-tuple-element.8) | data formatting | bytes 3538944
  107.5 6.2 %copy.122 = bf16[12,144,1,8,64]{1,4,3,0,2:T(8,128)(2,1)} copy(bf16[12,144,1,8,64]{4,3,2,1,0:T(8,128)(2,1)} %get-tuple-element.9) | data formatting | bytes 3538944
  117.7 13.4 %fusion.168 = (f32[12,8,144]{2,1,0:T(8,128)S(1)}, f32[12,8,144,144]{2,3,1,0:T(8,128)}) fusion(pred[12,144,144]{1,2,0:T(8,128)(4,1)} %broadcast_compare_fusion, bf16[12,144,1,8,64]{1,4,3,0,2:T(8,128)(2,1)} %copy.122, bf16[12,144,1,8,64]{1,4,3,0,2:T(8,128)(2,1)} %copy.121), kind=kOutput, calls=%fused_computation.199 | convolution fusion | flops 262766736 | bytes 11805696 | tf_op jit(solution)/shard_map/sub | solution.py:88
  131.1 7.9 %convert_bitcast_fusion = bf16[12,144,8,64]{1,3,2,0:T(8,128)(2,1)} fusion(f32[12,8,144,144]{2,3,1,0:T(8,128)} %get-tuple-element.14, f32[12,8,144]{2,1,0:T(8,128)S(1)} %get-tuple-element.13, bf16[12,144,1,8,64]{1,4,3,0,2:T(8,128)(2,1)S(1)} %copy-done.2), kind=kOutput, calls=%fused_computation.76 | convolution fusion | flops 259670016 | bytes 11556864 | tf_op jit(solution)/shard_map/ghqk,gkhe->gqhe/dot_general | solution.py:90
  139.0 4.7 %copy.100 = bf16[12,144,8,64]{3,2,1,0:T(8,128)(2,1)S(1)} copy(bf16[12,144,8,64]{1,3,2,0:T(8,128)(2,1)} %convert_bitcast_fusion) | data formatting | bytes 3538944 | tf_op jit(solution)/shard_map/convert_element_type | solution.py:92
  147.3 5.1 %add_convert_fusion = bf16[1728,512]{1,0:T(8,128)(2,1)} fusion(f32[1728,512]{1,0:T(8,128)} %copy-done, bf16[1728,512]{1,0:T(8,128)(2,1)} %reshape.210, bf16[512,512]{1,0:T(8,128)(2,1)} %all_gather.28), kind=kOutput, calls=%fused_computation.67 | convolution fusion | flops 907739136 | bytes 7602176 | tf_op jit(solution)/shard_map/dot_general | solution.py:47
  158.7 13.1 %collective-permute-done.2 = bf16[2,3,72,512]{3,0,2,1:T(2,128)(2,1)S(1)} collective-permute-done((bf16[2,3,72,512]{3,0,2,1:T(2,128)(2,1)S(1)}, bf16[2,3,72,512]{3,0,2,1:T(2,128)(2,1)S(1)}, u32[]{:S(2)}, u32[]{:S(2)}) %collective-permute-start.2) | collective-permute-done | bytes 442400 | tf_op jit(solution)/shard_map/ppermute | solution.py:19
  193.6 38.1 %fusion.48 = f32[1728,512]{1,0:T(8,128)} fusion(bf16[2048,512]{1,0:T(8,128)(2,1)} %all-gather.13.cloned.1.call-done, bf16[1728,512]{1,0:T(8,128)(2,1)} %fusion.36, bf16[512,2048]{1,0:T(8,128)(2,1)} %all-gather.11.cloned.1.call-done, f32[2,12,72,512]{3,2,1,0:T(8,128)S(1)} %copy.102), kind=kOutput, calls=%fused_computation.77 | convolution fusion | flops 7480442880 | bytes 13041664 | tf_op jit(solution)/shard_map/dot_general | solution.py:47
  235.8 4.5 %copy.139 = f32[2,6,2,36,2,512]{5,2,4,3,1,0:T(2,128)} copy(f32[2,6,2,36,2,512]{5,4,3,2,1,0:T(2,128)S(1)} %reshape.223) | data formatting | bytes 7077888 | tf_op jit(solution)/shard_map/convert_element_type | solution.py:23
  243.6 6.6 %multiply_reduce_fusion.1 = f32[2,6,36]{2,1,0:T(8,128)S(1)} fusion(f32[2,6,36]{2,1,0:T(8,128)S(1)} %broadcast_multiply_fusion.3, f32[2,6,2,36,2,512]{5,4,3,2,1,0:T(2,128)S(1)} %reshape.223), kind=kLoop, calls=%fused_computation.65 | loop fusion | flops 2653776 | bytes 3542400 | tf_op jit(solution)/shard_map/reduce_sum | solution.py:25
  250.4 4.7 %reshape.217 = f32[432,2048]{1,0:T(8,128)S(1)} reshape(f32[2,6,36,2,2,512]{5,4,3,2,1,0:T(2,128)} %bitcast.96) | data formatting | bytes 7077888 | tf_op jit(solution)/shard_map/convert_element_type | solution.py:23
  255.1 5.5 %fusion.79 = f32[432,1024]{1,0:T(8,128)} fusion(bf16[2048,1024]{1,0:T(8,128)(2,1)} %all-gather.15.cloned.1.call-done, f32[432,2048]{1,0:T(8,128)S(1)} %reshape.217, f32[2048]{0:T(1024)} %param.22, f32[432]{0:T(512)S(1)} %rsqrt.57, f32[432]{0:T(512)S(1)} %div.63), kind=kOutput, calls=%fused_computation.109 | convolution fusion | flops 1816363008 | bytes 9514368 | tf_op jit(solution)/shard_map/dot_general | solution.py:47
  267.7 6.4 %convolution_convert_fusion.1 = bf16[432,3072]{1,0:T(8,128)(2,1)S(1)} fusion(bf16[1024,3072]{1,0:T(8,128)(2,1)} %all-gather.17.cloned.1.call-done, f32[432,1024]{1,0:T(8,128)} %reshape.218, f32[1024]{0:T(1024)S(1)} %copy-done.5, f32[432]{0:T(512)S(1)} %rsqrt.59, f32[432]{0:T(512)S(1)} %div.66), kind=kOutput, calls=%fused_computation.54 | convolution fusion | flops 2721005568 | bytes 10722688 | tf_op jit(solution)/shard_map/dot_general | solution.py:47
  274.1 5.0 %reshape.212 = bf16[3,144,3,16,64]{4,3,2,1,0:T(8,128)(2,1)} reshape(bf16[432,3072]{1,0:T(8,128)(2,1)S(1)} %convolution_convert_fusion.1) | data formatting | bytes 5308416 | tf_op jit(solution)/shard_map/reshape | solution.py:77
  279.1 5.6 %fusion.167 = (bf16[3,144,1,16,64]{4,3,2,1,0:T(8,128)(2,1)}, bf16[3,144,1,16,64]{4,3,2,1,0:T(8,128)(2,1)S(1)}, bf16[3,144,1,16,64]{4,3,2,1,0:T(8,128)(2,1)}) fusion(bf16[3,144,3,16,64]{4,3,2,1,0:T(8,128)(2,1)} %reshape.212), kind=kLoop, calls=%fused_computation.198 | loop fusion | bytes 5308416 | tf_op jit(solution)/shard_map/slice | solution.py:91
  294.7 6.7 %fusion.173 = (f32[3,16,144]{2,1,0:T(8,128)S(1)}, f32[3,16,144,144]{2,3,1,0:T(8,128)S(1)}) fusion(f32[3,16,144,144]{2,3,1,0:T(8,128)S(1)} %fusion.69), kind=kOutput, calls=%fused_computation.200 | output fusion | flops 3981455 | bytes 7990272 | tf_op jit(solution)/shard_map/sub | solution.py:88
  312.2 51.3 %all-gather.23.cloned.1.call-done = bf16[4096,1024]{1,0:T(8,128)(2,1)} async-done(((bf16[256,1024]{1,0:T(8,128)(2,1)}), bf16[4096,1024]{1,0:T(8,128)(2,1)}) %all-gather.23.cloned.1.call-update) | async-done | bytes 8388624 | tf_op jit(solution)/shard_map/all_gather | solution.py:48
  363.5 26.2 %fusion.58 = bf16[432,1024]{1,0:T(8,128)(2,1)S(1)} fusion(bf16[432,1024]{1,0:T(8,128)(2,1)S(1)} %get-tuple-element.18, bf16[4096,1024]{1,0:T(8,128)(2,1)} %all-gather.23.cloned.1.call-done, bf16[1024,4096]{1,0:T(8,128)(2,1)} %all-gather.21.cloned.1.call-done, f32[1024]{0:T(1024)S(1)} %copy-done.6, f32[432]{0:T(512)S(1)} %add_rsqrt_fusion.4, ...), kind=kOutput, calls=%fused_computation.87 | convolution fusion | flops 7366311936 | bytes 18554240 | tf_op jit(solution)/shard_map/dot_general | solution.py:47
  (109 shorter events, 103.3 us)
Async XLA Ops:
  6.5 67.8 %all-gather.9.cloned.1.call-start = ((), (), s32[]{:S(2)}) async-start(), calls=%async_computation | async-start | bytes 1671168 | tf_op jit(solution)/shard_map/all_gather | solution.py:48
  7.3 186.4 %all-gather.11.cloned.1.call-start = ((), (), s32[]{:S(2)}) async-start(), calls=%async_computation.1 | async-start | bytes 2228224 | tf_op jit(solution)/shard_map/all_gather | solution.py:48
  8.0 185.6 %all-gather.13.cloned.1.call-start = ((), (), s32[]{:S(2)}) async-start(), calls=%async_computation.2 | async-start | bytes 2228224 | tf_op jit(solution)/shard_map/all_gather | solution.py:48
  8.7 246.3 %all-gather.15.cloned.1.call-start = ((), (), s32[]{:S(2)}) async-start(), calls=%async_computation.3 | async-start | bytes 4456448 | tf_op jit(solution)/shard_map/all_gather | solution.py:48
  9.3 258.4 %all-gather.17.cloned.1.call-start = ((), (), s32[]{:S(2)}) async-start(), calls=%async_computation.4 | async-start | bytes 6684672 | tf_op jit(solution)/shard_map/all_gather | solution.py:48
  9.9 298.8 %all-gather.19.cloned.1.call-start = ((), (), s32[]{:S(2)}) async-start(), calls=%async_computation.5 | async-start | bytes 2228224 | tf_op jit(solution)/shard_map/all_gather | solution.py:48
  10.5 301.7 %all-gather.21.cloned.1.call-start = ((), (), s32[]{:S(2)}) async-start(), calls=%async_computation.6 | async-start | bytes 8912896 | tf_op jit(solution)/shard_map/all_gather | solution.py:48
  11.2 352.2 %all-gather.23.cloned.1.call-start = ((), (), s32[]{:S(2)}) async-start(), calls=%async_computation.7 | async-start | bytes 8912896 | tf_op jit(solution)/shard_map/all_gather | solution.py:48
  12.3 34.8 %collective-permute-start = (bf16[2,3,72,512]{3,2,1,0:T(8,128)(2,1)S(1)}, bf16[2,3,72,512]{3,2,1,0:T(8,128)(2,1)S(1)}, u32[]{:S(2)}, u32[]{:S(2)}) collective-permute-start(bf16[2,3,72,512]{3,2,1,0:T(8,128)(2,1)S(1)} %slice.43), channel_id=1, source_target_pairs={{0,112},{16,0},{32,16},{48,32},{64,48},{80,64},{96,80},{112,96},{1... | collective-permute-start | bytes 1327112 | tf_op jit(solution)/shard_map/ppermute | solution.py:19
  47.2 5.7 %collective-permute-start.1 = (bf16[2,12,6,512]{3,2,1,0:T(8,128)(2,1)S(1)}, bf16[2,12,6,512]{3,2,1,0:T(8,128)(2,1)S(1)}, u32[]{:S(2)}, u32[]{:S(2)}) collective-permute-start(bf16[2,12,6,512]{3,2,1,0:T(8,128)(2,1)S(1)} %pad_maximum_fusion.1), channel_id=1, source_target_pairs={{0,15},{1,0},{2,1},{3,2},{4,3},{5,4},{6,5},{7,6},{8,7},{9,8},{10,9... | collective-permute-start | bytes 442376 | tf_op jit(solution)/shard_map/ppermute | solution.py:19
  73.2 7.8 %copy-start = (f32[1728,512]{1,0:T(8,128)}, f32[1728,512]{1,0:T(8,128)S(1)}, u32[]{:S(2)}) copy-start(f32[1728,512]{1,0:T(8,128)S(1)} %reshape.215) | copy-start | bytes 10616836
  117.7 13.4 %copy-start.2 = (bf16[12,144,1,8,64]{1,4,3,0,2:T(8,128)(2,1)S(1)}, bf16[12,144,1,8,64]{1,4,3,0,2:T(8,128)(2,1)}, u32[]{:S(2)}) copy-start(bf16[12,144,1,8,64]{1,4,3,0,2:T(8,128)(2,1)} %copy.120) | copy-start | bytes 5308420
  157.0 14.7 %collective-permute-start.2 = (bf16[2,3,72,512]{3,0,2,1:T(2,128)(2,1)S(1)}, bf16[2,3,72,512]{3,0,2,1:T(2,128)(2,1)S(1)}, u32[]{:S(2)}, u32[]{:S(2)}) collective-permute-start(bf16[2,3,72,512]{3,0,2,1:T(2,128)(2,1)S(1)} %slice.61), channel_id=1, source_target_pairs={{0,16},{16,32},{32,48},{48,64},{64,80},{80,96},{96,112},{112,0},{1... | collective-permute-start | bytes 1327112 | tf_op jit(solution)/shard_map/ppermute | solution.py:19
  171.9 3.4 collective-permute-start.3
  179.6 1.1 copy-start.1
  262.3 5.4 %copy-start.5 = (f32[1024]{0:T(1024)S(1)}, f32[1024]{0:T(1024)}, u32[]{:S(2)}) copy-start(f32[1024]{0:T(1024)} %param.24) | copy-start | bytes 12292
  294.7 6.7 %copy-start.4 = (bf16[3,144,1,16,64]{1,4,3,0,2:T(8,128)(2,1)S(1)}, bf16[3,144,1,16,64]{1,4,3,0,2:T(8,128)(2,1)}, u32[]{:S(2)}) copy-start(bf16[3,144,1,16,64]{1,4,3,0,2:T(8,128)(2,1)} %copy.123) | copy-start | bytes 2654212
  301.4 7.3 %copy-start.3 = (f32[432,1024]{1,0:T(8,128)S(1)}, f32[432,1024]{1,0:T(8,128)}, u32[]{:S(2)}) copy-start(f32[432,1024]{1,0:T(8,128)} %reshape.218) | copy-start | bytes 5308420
  306.4 57.0 %copy-start.6 = (f32[1024]{0:T(1024)S(1)}, f32[1024]{0:T(1024)}, u32[]{:S(2)}) copy-start(f32[1024]{0:T(1024)} %param.27) | copy-start | bytes 12292
Sparse Core Ops, SparseCore 0:
  9.1 45.2 all-gather.8
  56.1 33.6 all-gather.10
  91.5 34.2 all-gather.12
  127.4 38.5 all-gather.14
  167.6 50.7 all-gather.16
  220.0 34.8 all-gather.18
  256.5 52.1 all-gather.20
  310.4 52.9 all-gather.22
where the time goes:
time: 407 us; the launch traced here: 399 us
  local copies, waits for them, and re-layouts  119 us (29%)
  matrix products  115 us (28%)
  waiting for transfers between devices  75.9 us (19%)
  other arithmetic  39.7 us (10%)
  blocking collectives  25.4 us (6%)
  between operations  14.4 us (4%)
  starting transfers between devices  9.11 us (2%)
    dot_general x7, matrix products, project(): jnp.dot(values, lax.all_gather(shard, 'lon', axis=0, tiled=True), preferr...  90.9 us
    all_gather x8, waiting for transfers between devices, project(): lax.all_gather(shard, 'lon', axis=0, tiled=True)  51.4 us
    unnamed x20, local copies, waits for them, and re-layouts  25.7 us
    all_gather x1, blocking collectives, project(): lax.all_gather(shard, 'lon', axis=0, tiled=True)  25.4 us
    ppermute x4, waiting for transfers between devices, passed_along(): return lax.ppermute(value, axis, pairs)  20.2 us
    reshape x2, local copies, waits for them, and re-layouts, attend(): linear(normed, 0).astype(jnp.bfloat16)  19 us
    convert_element_type x6, local copies, waits for them, and re-layouts, attend(): flat.astype(jnp.float32) + linear(context.reshape(-1, width), 1)  15.1 us
    reduce_sum x5, other arithmetic, layer_norm(): spread = jnp.mean(center * center, -1, keepdims=True)  14.6 us
  transfers between devices with their start and end apart: 12, of which 4 were waited for; matrix products, arithmetic and copies ran while one was open for 62% of the time, Pallas kernels for 0%

commit v1 on v0

v1 whole, which is shorter than its diff:
```python
import functools
import jax
import jax.numpy as jnp
from jax import lax
from jax.experimental import pallas as pl
from jax.experimental.pallas import tpu as pltpu
from jax.sharding import Mesh, PartitionSpec as P

HEAD = 64
COUNT = 144
WIN_LEV = 2
WIN_LAT = 6
WIN_LON = 12
EPS = 1e-05
SCALE = 0.125
VMEM_LIMIT = 56 * 1024 * 1024
F32 = jnp.float32
BF16 = jnp.bfloat16


def normalize(values, gain):
    center = values - jnp.mean(values, -1, keepdims=True)
    spread = jnp.mean(center * center, -1, keepdims=True)
    return center * lax.rsqrt(spread + EPS) * gain


def dot(left, right):
    return jnp.dot(left, right, preferred_element_type=F32)


def gelu(x):
    return 0.5 * x * (1.0 + lax.erf(x * (0.5 ** 0.5)))


def fetch(order, buffers, place, semaphore):
    copies = []
    position = 0
    for buffer in buffers:
        for item in range(buffer.shape[0]):
            for source, target in place(buffer.at[item], order[position]):
                copies.append(pltpu.make_async_copy(source, target, semaphore))
            position += 1
    for copy in copies:
        copy.start()
    return copies


def await_all(copies):
    for copy in copies:
        copy.wait()


def attend_kernel(heads, windows, masked, order, x_ref, bias_ref, gain_ref, *rest):
    *buffers, out_ref, weights, qkv, context, semaphore = rest
    width = heads * HEAD
    share = width // 16
    first = pl.program_id(0) == 0

    @pl.when(first)
    def _():
        def place(block, index):
            rows = pl.ds(pl.multiple_of(index * share, share), share)
            return [(block, weights.at[:, rows, :])]

        await_all(fetch(order, buffers, place, semaphore))

    normed = normalize(x_ref[...].astype(F32), gain_ref[...]).astype(BF16)
    qkv[:, :width] = (dot(normed, weights[0]) * SCALE).astype(BF16)
    qkv[:, width : 2 * width] = dot(normed, weights[1]).astype(BF16)
    qkv[:, 2 * width :] = dot(normed, weights[2]).astype(BF16)

    low = lax.broadcasted_iota(jnp.int32, (COUNT, 128), 1) < HEAD
    zero = jnp.zeros((COUNT, 128), BF16)
    one = jnp.ones((COUNT, 128), BF16)

    def window(index, _):
        rows = pl.ds(pl.multiple_of(index * COUNT, COUNT), COUNT)
        for pair in range(heads // 2):
            lanes = slice(pair * 128, pair * 128 + 128)
            q = qkv[rows, lanes]
            k = qkv[rows, width + pair * 128 : width + pair * 128 + 128]
            v = qkv[rows, 2 * width + pair * 128 : 2 * width + pair * 128 + 128]
            results = []
            for half in range(2):
                mine = low if half == 0 else jnp.logical_not(low)
                scores = lax.dot_general(
                    q, jnp.where(mine, k, zero), (((1,), (1,)), ((), ())), preferred_element_type=F32
                )
                if masked:
                    scores = scores + bias_ref[...]
                powers = jnp.exp(scores - jnp.max(scores, -1, keepdims=True)).astype(BF16)
                results.append(dot(powers, jnp.where(mine, v, one)))
            upper = jnp.where(low, results[0], results[1])
            lower = jnp.where(low, results[1], results[0])
            context[rows, lanes] = (upper / pltpu.roll(lower, HEAD, 1)).astype(BF16)
        return 0

    lax.fori_loop(0, windows, window, 0)
    out_ref[...] = (x_ref[...].astype(F32) + dot(context[...], weights[3])).astype(BF16)


def any_specs(buffers):
    return [pl.BlockSpec(memory_space=pl.ANY)] * len(buffers)


def params():
    return pltpu.CompilerParams(
        dimension_semantics=("arbitrary",), vmem_limit_bytes=VMEM_LIMIT
    )


def attend(x, bias, gain, order, buffers, heads, steps):
    tokens, width = x.shape
    tile = tokens // steps
    masked = bias is not None
    if not masked:
        bias = jnp.zeros((1, COUNT, COUNT), F32)
    picks = bias.shape[0] > 1
    return pl.pallas_call(
        functools.partial(attend_kernel, heads, tile // COUNT, masked),
        out_shape=jax.ShapeDtypeStruct(x.shape, BF16),
        grid=(steps,),
        in_specs=[
            pl.BlockSpec(memory_space=pltpu.SMEM),
            pl.BlockSpec((tile, width), lambda i: (i, 0)),
            pl.BlockSpec((None, COUNT, COUNT), lambda i: (i if picks else 0, 0, 0)),
            pl.BlockSpec((1, width), lambda i: (0, 0)),
        ]
        + any_specs(buffers),
        out_specs=pl.BlockSpec((tile, width), lambda i: (i, 0)),
        scratch_shapes=[
            pltpu.VMEM((4, width, width), BF16),
            pltpu.VMEM((tile, 3 * width), BF16),
            pltpu.VMEM((tile, width), BF16),
            pltpu.SemaphoreType.DMA,
        ],
        compiler_params=params(),
        cost_estimate=pl.CostEstimate(
            flops=8 * tokens * width * width + 4 * tokens * COUNT * width,
            bytes_accessed=8 * width * width + 4 * tokens * width,
            transcendentals=tokens * COUNT * heads,
        ),
    )(order, x, bias, gain.reshape(1, -1), *buffers)


def dense_kernel(order, x_ref, gain_ref, *rest):
    *buffers, out_ref, expand, shrink, semaphore = rest
    width = x_ref.shape[1]
    share = width // 16

    @pl.when(pl.program_id(0) == 0)
    def _():
        def place(block, index):
            rows = pl.ds(pl.multiple_of(index * share, share), share)
            return [
                (block.at[pl.ds(0, 4)], expand.at[:, rows, :]),
                (block.at[pl.ds(4, 4)], shrink.at[pl.ds(index * 4, 4)]),
            ]

        await_all(fetch(order, buffers, place, semaphore))

    x = x_ref[...].astype(F32)
    hidden = normalize(x, gain_ref[...]).astype(BF16)
    total = x
    for part in range(4):
        grown = gelu(dot(hidden, expand[part])).astype(BF16)
        back = shrink[part * 16 : part * 16 + 16].reshape(width, width)
        total = total + dot(grown, back)
    out_ref[...] = total.astype(BF16)


def dense(x, gain, order, buffers, steps):
    tokens, width = x.shape
    tile = tokens // steps
    return pl.pallas_call(
        dense_kernel,
        out_shape=jax.ShapeDtypeStruct(x.shape, BF16),
        grid=(steps,),
        in_specs=[
            pl.BlockSpec(memory_space=pltpu.SMEM),
            pl.BlockSpec((tile, width), lambda i: (i, 0)),
            pl.BlockSpec((1, width), lambda i: (0, 0)),
        ]
        + any_specs(buffers),
        out_specs=pl.BlockSpec((tile, width), lambda i: (i, 0)),
        scratch_shapes=[
            pltpu.VMEM((4, width, width), BF16),
            pltpu.VMEM((64, width // 16, width), BF16),
            pltpu.SemaphoreType.DMA,
        ],
        compiler_params=params(),
        cost_estimate=pl.CostEstimate(
            flops=16 * tokens * width * width,
            bytes_accessed=16 * width * width + 4 * tokens * width,
            transcendentals=4 * tokens * width,
        ),
    )(order, x, gain.reshape(1, -1), *buffers)


def merge_kernel(order, x_ref, gain_ref, *rest):
    *buffers, out_ref, weights, semaphore = rest
    width = x_ref.shape[2]

    def place(block, index):
        return [(block, weights.at[pl.ds(index * 2, 2)])]

    copies = fetch(order, buffers, place, semaphore)
    quarters = [x_ref[part].astype(F32) for part in range(4)]
    mean = sum(jnp.sum(item, -1, keepdims=True) for item in quarters) / (4 * width)
    quarters = [item - mean for item in quarters]
    spread = sum(jnp.sum(item * item, -1, keepdims=True) for item in quarters) / (4 * width)
    level = lax.rsqrt(spread + EPS)
    normed = [
        (item * level * gain_ref[:, part * width : part * width + width]).astype(BF16)
        for part, item in enumerate(quarters)
    ]
    await_all(copies)
    total = dot(normed[0], weights[0:8].reshape(width, 2 * width))
    for part in range(1, 4):
        total = total + dot(normed[part], weights[part * 8 : part * 8 + 8].reshape(width, 2 * width))
    out_ref[...] = total.astype(BF16)


def merge(x, gain, order, buffers):
    _, tokens, width = x.shape
    return pl.pallas_call(
        merge_kernel,
        out_shape=jax.ShapeDtypeStruct((tokens, 2 * width), BF16),
        in_specs=[
            pl.BlockSpec(memory_space=pltpu.SMEM),
            pl.BlockSpec(memory_space=pltpu.VMEM),
            pl.BlockSpec(memory_space=pltpu.VMEM),
        ]
        + any_specs(buffers),
        out_specs=pl.BlockSpec(memory_space=pltpu.VMEM),
        scratch_shapes=[
            pltpu.VMEM((32, width // 8, 2 * width), BF16),
            pltpu.SemaphoreType.DMA,
        ],
        compiler_params=pltpu.CompilerParams(vmem_limit_bytes=VMEM_LIMIT),
        cost_estimate=pl.CostEstimate(
            flops=16 * tokens * width * width,
            bytes_accessed=16 * width * width + 12 * tokens * width,
            transcendentals=0,
        ),
    )(order, x, gain.reshape(1, -1), *buffers)


def grow_kernel(order, x_ref, gain_ref, *rest):
    *buffers, out_ref, weights, semaphore = rest
    width = x_ref.shape[1]
    share = width // 16

    def place(block, index):
        rows = pl.ds(pl.multiple_of(index * share, share), share)
        return [(block, weights.at[:, rows, :])]

    copies = fetch(order, buffers, place, semaphore)
    hidden = normalize(x_ref[...].astype(F32), gain_ref[...]).astype(BF16)
    await_all(copies)
    for part in range(4):
        for half in range(2):
            lanes = slice(half * (width // 2), (half + 1) * (width // 2))
            target = slice(part * width + half * (width // 2), part * width + (half + 1) * (width // 2))
            out_ref[:, target] = gelu(dot(hidden, weights[part, :, lanes])).astype(BF16)


def grow(x, gain, order, buffers):
    tokens, width = x.shape
    return pl.pallas_call(
        grow_kernel,
        out_shape=jax.ShapeDtypeStruct((tokens, 4 * width), BF16),
        in_specs=[
            pl.BlockSpec(memory_space=pltpu.SMEM),
            pl.BlockSpec(memory_space=pltpu.VMEM),
            pl.BlockSpec(memory_space=pltpu.VMEM),
        ]
        + any_specs(buffers),
        out_specs=pl.BlockSpec(memory_space=pltpu.VMEM),
        scratch_shapes=[pltpu.VMEM((4, width, width), BF16), pltpu.SemaphoreType.DMA],
        compiler_params=pltpu.CompilerParams(vmem_limit_bytes=VMEM_LIMIT),
        cost_estimate=pl.CostEstimate(
            flops=8 * tokens * width * width,
            bytes_accessed=8 * width * width + 10 * tokens * width,
            transcendentals=4 * tokens * width,
        ),
    )(order, x, gain.reshape(1, -1), *buffers)


def fold_kernel(order, x_ref, grown_ref, *rest):
    *buffers, out_ref, weights, semaphore = rest
    width = x_ref.shape[1]

    def place(block, index):
        return [(block, weights.at[pl.ds(index * 4, 4)])]

    await_all(fetch(order, buffers, place, semaphore))
    for half in range(2):
        lanes = slice(half * (width // 2), (half + 1) * (width // 2))
        back = weights[:, :, lanes].reshape(4 * width, width // 2)
        out_ref[:, lanes] = (x_ref[:, lanes].astype(F32) + dot(grown_ref[...], back)).astype(BF16)


def fold(x, grown, order, buffers):
    tokens, width = x.shape
    return pl.pallas_call(
        fold_kernel,
        out_shape=jax.ShapeDtypeStruct((tokens, width), BF16),
        in_specs=[
            pl.BlockSpec(memory_space=pltpu.SMEM),
            pl.BlockSpec(memory_space=pltpu.VMEM),
            pl.BlockSpec(memory_space=pltpu.VMEM),
        ]
        + any_specs(buffers),
        out_specs=pl.BlockSpec(memory_space=pltpu.VMEM),
        scratch_shapes=[pltpu.VMEM((64, width // 16, width), BF16), pltpu.SemaphoreType.DMA],
        compiler_params=pltpu.CompilerParams(vmem_limit_bytes=VMEM_LIMIT),
        cost_estimate=pl.CostEstimate(
            flops=8 * tokens * width * width,
            bytes_accessed=8 * width * width + 12 * tokens * width,
            transcendentals=0,
        ),
    )(order, x, grown, *buffers)


def gather(shard):
    whole = lax.all_gather(shard, ("y", "zl", "c"), axis=0, tiled=False)
    return whole


def in_columns(shard, parts):
    rows, columns = shard.shape
    return shard.reshape(rows, parts, columns // parts).transpose(1, 0, 2)


def in_rows(shard, parts):
    rows, columns = shard.shape
    return shard.reshape(parts, rows // parts, columns)


def passed_along(value, axes, steps):
    count = 1
    for axis in axes:
        count *= lax.axis_size(axis)
    pairs = [(source, (source + steps) % count) for source in range(count)]
    return lax.ppermute(value, axes, pairs)


LAT = ("x", "zh")
LON = ("y", "zl", "c")


def roll_lat(grid, forward):
    cut = WIN_LAT // 2
    height = grid.shape[1]
    edge = grid[:, :cut] if forward else grid[:, height - cut :]
    moved = passed_along(edge, LAT, -1 if forward else 1)
    if forward:
        return jnp.concatenate([grid[:, cut:], moved], 1)
    return jnp.concatenate([moved, grid[:, : height - cut]], 1)


def roll_lon(grid, forward):
    cut = WIN_LON // 2
    breadth = grid.shape[2]
    edge = grid[:, :, :cut] if forward else grid[:, :, breadth - cut :]
    moved = passed_along(edge, LON, -1 if forward else 1)
    if forward:
        return jnp.concatenate([grid[:, :, cut:], moved], 2)
    return jnp.concatenate([moved, grid[:, :, : breadth - cut]], 2)


def window_split(grid):
    levels, rows, cols, width = grid.shape
    parts = grid.reshape(levels, rows // WIN_LAT, WIN_LAT, cols // WIN_LON, WIN_LON, width)
    return parts.transpose(1, 3, 0, 2, 4, 5).reshape(-1, width)


def window_join(parts, rows, cols):
    width = parts.shape[-1]
    grid = parts.reshape(rows // WIN_LAT, cols // WIN_LON, WIN_LEV, WIN_LAT, WIN_LON, width)
    return grid.transpose(2, 0, 3, 1, 4, 5).reshape(WIN_LEV, rows, cols, width)


def per_device(
    latents,
    attend_gain,
    packed_heads,
    heads_back,
    dense_gain,
    expand_weight,
    shrink_weight,
    merge_gain,
    merge_weight,
    coarse_gain,
    coarse_heads,
    coarse_back,
    coarse_scale,
    coarse_expand,
    coarse_shrink,
):
    _, rows, cols, width = latents.shape
    order = jnp.arange(16, dtype=jnp.int32)
    fine_attend = [gather(jnp.concatenate([in_columns(packed_heads, 3), heads_back[None]], 0))]
    fine_dense = [gather(jnp.concatenate([in_columns(expand_weight, 4), in_rows(shrink_weight, 4)], 0))]
    merging = [gather(in_rows(merge_weight, 2))]
    coarse_attend = [gather(jnp.concatenate([in_columns(coarse_heads, 3), coarse_back[None]], 0))]
    coarse_grow = [gather(in_columns(coarse_expand, 4))]
    coarse_fold = [gather(in_rows(coarse_shrink, 4))]

    rolled = roll_lon(roll_lat(latents, True), True)
    late = (jnp.arange(COUNT) // WIN_LON) % WIN_LAT >= WIN_LAT // 2
    wall = jnp.where(late[:, None] == late[None, :], 0.0, -1e30).astype(F32)
    place = lax.axis_index("x") * 2 + lax.axis_index("zh")
    last = (place == lax.axis_size("x") * 2 - 1).astype(F32)
    bias = jnp.stack([jnp.zeros_like(wall), wall * last])

    mixed = attend(window_split(rolled), bias, attend_gain, order, fine_attend, 8, 2)
    shifted = dense(mixed, dense_gain, order, fine_dense, 4)
    first = roll_lon(roll_lat(window_join(shifted, rows, cols), False), False)
    quads = first.reshape(WIN_LEV, rows // 2, 2, cols // 24, WIN_LON, 2, width)
    quads = quads.transpose(5, 2, 3, 0, 1, 4, 6).reshape(4, -1, width)
    merged = merge(quads, merge_gain, order, merging)
    coarse_mixed = attend(merged, None, coarse_gain, order, coarse_attend, 16, 1)
    grown = grow(coarse_mixed, coarse_scale, order, coarse_grow)
    finished = fold(coarse_mixed, grown, order, coarse_fold)
    return window_join(finished, rows // 2, cols // 2)


def solution(mesh):
    fine_mesh = Mesh(mesh.devices.reshape(4, 2, 4, 2, 2), ("x", "zh", "y", "zl", "c"))
    rows = P(LON, None)
    grid = P(None, LAT, LON, None)
    in_specs = (grid, P(), rows, rows, P(), rows, rows, P(), rows, P(), rows, rows, P(), rows, rows)
    return jax.shard_map(
        per_device, mesh=fine_mesh, in_specs=in_specs, out_specs=grid, check_vma=False
    )
```

time: 407 us -> 328 us (0.81); the launches traced: 399 us -> 328 us
  matrix products: 115 us -> 0 us
  waiting for transfers between devices: 75.9 us -> 189 us
  local copies, waits for them, and re-layouts: 119 us -> 29.2 us
  Pallas kernels: 0 us -> 76.1 us
  other arithmetic: 39.7 us -> 5.91 us
  blocking collectives: 25.4 us -> 0 us
    dot_general x10 -> x0, matrix products: 102 us -> none  [the longest x7 90.9 us: project(): jnp.dot(values, lax.all_gather(shard, 'lon', axis=0, tiled=True), preferr...]
    all_gather x8 -> x6, waiting for transfers between devices: 51.4 us -> 149 us  [gather(): whole = lax.all_gather(shard, ('y', 'zl', 'c'), axis=0, tiled=False)]
    pallas_call x0 -> x6, Pallas kernels: none -> 76.1 us  [the longest x2 34.4 us: attend(): pl.pallas_call(functools.partial(attend_kernel, heads, tile // COUNT, mas...]
    convert_element_type x12 -> x0, local copies, waits for them, and re-layouts: 36.8 us -> none  [the longest x6 15.1 us: attend(): flat.astype(jnp.float32) + linear(context.reshape(-1, width), 1)]
    unnamed x20 -> x8, local copies, waits for them, and re-layouts: 25.7 us -> 0.02 us
    all_gather x1 -> x0, blocking collectives: 25.4 us -> none  [project(): lax.all_gather(shard, 'lon', axis=0, tiled=True)]
    reduce_sum x9 -> x0, other arithmetic: 24.1 us -> none  [the longest x5 14.6 us: layer_norm(): spread = jnp.mean(center * center, -1, keepdims=True)]
    ppermute x4, waiting for transfers between devices: 20.2 us -> 38.7 us  [passed_along(): return lax.ppermute(value, axes, pairs)]
  transfers between devices with their start and end apart: 12 -> 10, of which waited for: 4 -> 9; matrix products, arithmetic and copies ran while one was open for 62% -> 9% of each run, Pallas kernels for 0% -> 20%
where the time goes in v1:
time: 328 us
  waiting for transfers between devices  189 us (58%)
  Pallas kernels  76.1 us (23%)
  local copies, waits for them, and re-layouts  29.2 us (9%)
  between operations  13.7 us (4%)
  starting transfers between devices  13.1 us (4%)
  other arithmetic  5.91 us (2%)
    all_gather x6, waiting for transfers between devices, gather(): whole = lax.all_gather(shard, ('y', 'zl', 'c'), axis=0, tiled=False)  149 us
    ppermute x4, waiting for transfers between devices, passed_along(): return lax.ppermute(value, axes, pairs)  38.7 us
    pallas_call x2, Pallas kernels, attend(): pl.pallas_call(functools.partial(attend_kernel, heads, tile // COUNT, mas...  34.4 us
    pallas_call x1, Pallas kernels, dense(): pl.pallas_call(dense_kernel, out_shape=jax.ShapeDtypeStruct(x.shape, BF16...  14 us
    ppermute x4, starting transfers between devices, passed_along(): return lax.ppermute(value, axes, pairs)  12.9 us
    pallas_call x1, Pallas kernels, grow(): pl.pallas_call(grow_kernel, out_shape=jax.ShapeDtypeStruct((tokens, 4 * w...  10.7 us
    pallas_call x1, Pallas kernels, fold(): pl.pallas_call(fold_kernel, out_shape=jax.ShapeDtypeStruct((tokens, width...  10.4 us
  transfers between devices with their start and end apart: 10, of which 9 were waited for; matrix products, arithmetic and copies ran while one was open for 9% of the time, Pallas kernels for 20%

profile of v1, /device:TPU:1, one launch (start us, length us, event | category | flops | bytes accessed | tf_op | source)
XLA Modules:
  0.0 327.5 jit_solution(14499620656805781442)
XLA Ops:
  18.2 6.6 %collective-permute-start = (bf16[2,3,72,512]{3,2,1,0:T(8,128)(2,1)}, bf16[2,3,72,512]{3,2,1,0:T(8,128)(2,1)S(1)}, u32[]{:S(2)}, u32[]{:S(2)}) collective-permute-start(bf16[2,3,72,512]{3,2,1,0:T(8,128)(2,1)} %slice.25), channel_id=1, source_target_pairs={{0,112},{16,0},{32,16},{48,32},{64,48},{80,64},{96,80},{112,96},{1... | collective-permute-start | bytes 1327112 | tf_op jit(solution)/shard_map/ppermute | solution.py:346
  25.8 12.6 %collective-permute-done = bf16[2,3,72,512]{3,2,1,0:T(8,128)(2,1)S(1)} collective-permute-done((bf16[2,3,72,512]{3,2,1,0:T(8,128)(2,1)}, bf16[2,3,72,512]{3,2,1,0:T(8,128)(2,1)S(1)}, u32[]{:S(2)}, u32[]{:S(2)}) %collective-permute-start) | collective-permute-done | bytes 442400 | tf_op jit(solution)/shard_map/ppermute | solution.py:346
  38.4 2.0 collective-permute-start.1
  40.8 6.2 %collective-permute-done.1 = bf16[2,12,6,512]{3,2,1,0:T(8,128)(2,1)S(1)} collective-permute-done((bf16[2,12,6,512]{3,2,1,0:T(8,128)(2,1)S(1)}, bf16[2,12,6,512]{3,2,1,0:T(8,128)(2,1)S(1)}, u32[]{:S(2)}, u32[]{:S(2)}) %collective-permute-start.1) | collective-permute-done | bytes 147488 | tf_op jit(solution)/shard_map/ppermute | solution.py:346
  49.6 1.9 reshape.144.x_ref
  51.5 4.0 %all-gather.15.cloned.1.call-done = bf16[64,32,512]{2,1,0:T(8,128)(2,1)} async-done(((bf16[4,32,512]{2,1,0:T(8,128)(2,1)}), bf16[64,32,512]{2,1,0:T(8,128)(2,1)}) %all-gather.15.cloned.1.call-update) | async-done | bytes 2097168 | tf_op jit(solution)/shard_map/all_gather | solution.py:327
  56.1 20.3 %shard_map.145.x_ref = bf16[1728,512]{1,0:T(8,128)(2,1)} custom-call(s32[16]{0:T(128)} %iota.24.order, bf16[1728,512]{1,0:T(8,128)(2,1)} %reshape.144.x_ref, f32[2,144,144]{2,1,0:T(8,128)} %stack.4.bias_ref, f32[1,512]{1,0:T(1,128)} %bitcast.50, bf16[16,4,32,512]{3,2,1,0:T(8,128)(2,1)} %bitcast.47), custom_call_target="tpu_custom_call" | custom-call | flops 4133486592 | bytes 5636096 | tf_op jit(solution)/shard_map/pallas_call | solution.py:119
  76.4 18.7 %all-gather.17.cloned.1.call-done = bf16[128,32,512]{2,1,0:T(8,128)(2,1)} async-done(((bf16[8,32,512]{2,1,0:T(8,128)(2,1)}), bf16[128,32,512]{2,1,0:T(8,128)(2,1)}) %all-gather.17.cloned.1.call-update) | async-done | bytes 4194320 | tf_op jit(solution)/shard_map/all_gather | solution.py:327
  95.6 14.0 %shard_map.146 = bf16[1728,512]{1,0:T(8,128)(2,1)} custom-call(s32[16]{0:T(128)} %iota.23.order, bf16[1728,512]{1,0:T(8,128)(2,1)} %shard_map.145.x_ref, f32[1,512]{1,0:T(1,128)} %bitcast.51, bf16[16,8,32,512]{3,2,1,0:T(8,128)(2,1)} %bitcast.46), custom_call_target="tpu_custom_call" | custom-call | flops 7247757312 | bytes 7733248 | tf_op jit(solution)/shard_map/pallas_call | solution.py:175
  109.7 2.4 reshape.150
  114.3 2.4 collective-permute-start.2
  117.7 17.8 %collective-permute-done.2 = bf16[2,3,72,512]{3,0,2,1:T(2,128)(2,1)S(1)} collective-permute-done((bf16[2,3,72,512]{3,0,2,1:T(2,128)(2,1)S(1)}, bf16[2,3,72,512]{3,0,2,1:T(2,128)(2,1)S(1)}, u32[]{:S(2)}, u32[]{:S(2)}) %collective-permute-start.2) | collective-permute-done | bytes 442400 | tf_op jit(solution)/shard_map/ppermute | solution.py:346
  135.6 2.0 collective-permute-start.3
  137.6 2.1 collective-permute-done.3
  139.7 4.1 %fusion = bf16[2,12,72,512]{3,0,2,1:T(2,128)(2,1)S(1)} fusion(bf16[2,9,72,512]{3,0,2,1:T(2,128)(2,1)S(1)} %slice.35, bf16[2,3,72,512]{3,0,2,1:T(2,128)(2,1)S(1)} %collective-permute-done.2, bf16[2,12,6,512]{3,0,2,1:T(2,128)(2,1)S(1)} %collective-permute-done.3), kind=kLoop, calls=%fused_computation.1 | loop fusion | flops 1769472 | bytes 3686400 | tf_op jit(solution)/shard_map/concatenate | solution.py:370
  144.4 2.0 reshape.165.x_ref
  146.9 6.5 %shard_map.147.x_ref = bf16[432,1024]{1,0:T(8,128)(2,1)} custom-call(s32[16]{0:T(128)} %iota.22.order, bf16[4,432,512]{2,1,0:T(8,128)(2,1)} %reshape.165.x_ref, f32[1,2048]{1,0:T(1,128)} %bitcast.43, bf16[16,2,64,1024]{3,2,1,0:T(8,128)(2,1)} %all-gather.11.cloned.1.call-done.rest_0_), custom_call_target="tpu_custom_call" | custom-call | flops 1811939328 | bytes 6848512 | tf_op jit(solution)/shard_map/pallas_call | solution.py:226
  153.4 44.0 %all-gather.19.cloned.1.call-done = bf16[64,64,1024]{2,1,0:T(8,128)(2,1)} async-done(((bf16[4,64,1024]{2,1,0:T(8,128)(2,1)}), bf16[64,64,1024]{2,1,0:T(8,128)(2,1)}) %all-gather.19.cloned.1.call-update) | async-done | bytes 8388624 | tf_op jit(solution)/shard_map/all_gather | solution.py:327
  198.6 14.2 %shard_map.148.x_ref = bf16[432,1024]{1,0:T(8,128)(2,1)} custom-call(s32[16]{0:T(128)} %iota.21.order, bf16[432,1024]{1,0:T(8,128)(2,1)} %shard_map.147.x_ref, f32[1,144,144]{2,1,0:T(8,128)} %broadcast_in_dim.16.bias_ref, f32[1,1024]{1,0:T(1,128)} %bitcast.48, bf16[16,4,64,1024]{3,2,1,0:T(8,128)(2,1)} %bitcast.44), custom_call_target="tpu_custom_call" | custom-call | flops 3878682624 | bytes 10158080 | tf_op jit(solution)/shard_map/pallas_call | solution.py:119
  212.8 39.3 %all-gather.21.cloned.1.call-done = bf16[64,64,1024]{2,1,0:T(8,128)(2,1)} async-done(((bf16[4,64,1024]{2,1,0:T(8,128)(2,1)}), bf16[64,64,1024]{2,1,0:T(8,128)(2,1)}) %all-gather.21.cloned.1.call-update) | async-done | bytes 8388624 | tf_op jit(solution)/shard_map/all_gather | solution.py:327
  252.6 10.7 %shard_map.149.grown_ref = bf16[432,4096]{1,0:T(8,128)(2,1)} custom-call(s32[16]{0:T(128)} %iota.26.order, bf16[432,1024]{1,0:T(8,128)(2,1)} %shard_map.148.x_ref, f32[1,1024]{1,0:T(1,128)} %bitcast.49, bf16[16,4,64,1024]{3,2,1,0:T(8,128)(2,1)} %bitcast.45), custom_call_target="tpu_custom_call" | custom-call | flops 3623878656 | bytes 12812288 | tf_op jit(solution)/shard_map/pallas_call | solution.py:270
  263.2 43.4 %all-gather.13.cloned.1.call-done.rest_0_ = bf16[16,4,64,1024]{3,2,1,0:T(8,128)(2,1)} async-done(((bf16[1,4,64,1024]{3,2,1,0:T(8,128)(2,1)}), bf16[16,4,64,1024]{3,2,1,0:T(8,128)(2,1)}) %all-gather.13.cloned.1.call-update) | async-done | bytes 8388624 | tf_op jit(solution)/shard_map/all_gather | solution.py:327
  307.2 10.4 %shard_map.150 = bf16[432,1024]{1,0:T(8,128)(2,1)} custom-call(s32[16]{0:T(128)} %iota.20.order, bf16[432,1024]{1,0:T(8,128)(2,1)} %shard_map.148.x_ref, bf16[432,4096]{1,0:T(8,128)(2,1)} %shard_map.149.grown_ref, bf16[16,4,64,1024]{3,2,1,0:T(8,128)(2,1)} %all-gather.13.cloned.1.call-done.rest_0_), custom_call_target="tpu_custom_call" | custom-call | flops 3623878656 | bytes 13697024 | tf_op jit(solution)/shard_map/pallas_call | solution.py:306
  318.8 1.8 copy.77
  (58 shorter events, 24.4 us)
Async XLA Ops:
  6.5 6.5 %copy-start.2 = (bf16[64,3072]{1,0:T(8,128)(2,1)S(1)}, bf16[64,3072]{1,0:T(8,128)(2,1)}, u32[]{:S(2)}) copy-start(bf16[64,3072]{1,0:T(8,128)(2,1)} %param.25) | copy-start | bytes 1179652
  6.5 49.1 %all-gather.15.cloned.1.call-start = ((), (), s32[]{:S(2)}) async-start(), calls=%async_computation.2 | async-start | bytes 2228224 | tf_op jit(solution)/shard_map/all_gather | solution.py:327
  8.5 5.1 %copy-start.3 = (bf16[64,1024]{1,0:T(8,128)(2,1)S(1)}, bf16[64,1024]{1,0:T(8,128)(2,1)}, u32[]{:S(2)}) copy-start(bf16[64,1024]{1,0:T(8,128)(2,1)} %param.26) | copy-start | bytes 393220
  9.2 85.9 %all-gather.17.cloned.1.call-start = ((), (), s32[]{:S(2)}) async-start(), calls=%async_computation.3 | async-start | bytes 4456448 | tf_op jit(solution)/shard_map/all_gather | solution.py:327
  12.2 134.1 %all-gather.11.cloned.1.call-start = ((), (), s32[]{:S(2)}) async-start(), calls=%async_computation | async-start | bytes 4456448 | tf_op jit(solution)/shard_map/all_gather | solution.py:327
  13.0 184.5 %all-gather.19.cloned.1.call-start = ((), (), s32[]{:S(2)}) async-start(), calls=%async_computation.4 | async-start | bytes 8912896 | tf_op jit(solution)/shard_map/all_gather | solution.py:327
  13.6 1.9 copy-start.1
  15.4 2.0 copy-start
  15.4 236.6 %all-gather.21.cloned.1.call-start = ((), (), s32[]{:S(2)}) async-start(), calls=%async_computation.5 | async-start | bytes 8912896 | tf_op jit(solution)/shard_map/all_gather | solution.py:327
  16.8 289.8 %all-gather.13.cloned.1.call-start = ((), (), s32[]{:S(2)}) async-start(), calls=%async_computation.1 | async-start | bytes 8912896 | tf_op jit(solution)/shard_map/all_gather | solution.py:327
  18.2 20.2 %collective-permute-start = (bf16[2,3,72,512]{3,2,1,0:T(8,128)(2,1)}, bf16[2,3,72,512]{3,2,1,0:T(8,128)(2,1)S(1)}, u32[]{:S(2)}, u32[]{:S(2)}) collective-permute-start(bf16[2,3,72,512]{3,2,1,0:T(8,128)(2,1)} %slice.25), channel_id=1, source_target_pairs={{0,112},{16,0},{32,16},{48,32},{64,48},{80,64},{96,80},{112,96},{1... | collective-permute-start | bytes 1327112 | tf_op jit(solution)/shard_map/ppermute | solution.py:346
  38.4 8.7 %collective-permute-start.1 = (bf16[2,12,6,512]{3,2,1,0:T(8,128)(2,1)S(1)}, bf16[2,12,6,512]{3,2,1,0:T(8,128)(2,1)S(1)}, u32[]{:S(2)}, u32[]{:S(2)}) collective-permute-start(bf16[2,12,6,512]{3,2,1,0:T(8,128)(2,1)S(1)} %pad_maximum_fusion.4), channel_id=1, source_target_pairs={{0,15},{1,0},{2,1},{3,2},{4,3},{5,4},{6,5},{7,6},{8,7},{9,8},{10,9... | collective-permute-start | bytes 442376 | tf_op jit(solution)/shard_map/ppermute | solution.py:346
  114.3 21.1 %collective-permute-start.2 = (bf16[2,3,72,512]{3,0,2,1:T(2,128)(2,1)S(1)}, bf16[2,3,72,512]{3,0,2,1:T(2,128)(2,1)S(1)}, u32[]{:S(2)}, u32[]{:S(2)}) collective-permute-start(bf16[2,3,72,512]{3,0,2,1:T(2,128)(2,1)S(1)} %slice.34), channel_id=1, source_target_pairs={{0,16},{16,32},{32,48},{48,64},{64,80},{80,96},{96,112},{112,0},{1... | collective-permute-start | bytes 1327112 | tf_op jit(solution)/shard_map/ppermute | solution.py:346
  135.6 4.1 %collective-permute-start.3 = (bf16[2,12,6,512]{3,0,2,1:T(2,128)(2,1)S(1)}, bf16[2,12,6,512]{3,0,2,1:T(2,128)(2,1)S(1)}, u32[]{:S(2)}, u32[]{:S(2)}) collective-permute-start(bf16[2,12,6,512]{3,0,2,1:T(2,128)(2,1)S(1)} %pad_maximum_fusion.5), channel_id=1, source_target_pairs={{0,1},{1,2},{2,3},{3,4},{4,5},{5,6},{6,7},{7,8},{8,9},{9,10},{10,1... | collective-permute-start | bytes 442376 | tf_op jit(solution)/shard_map/ppermute | solution.py:346
Sparse Core Ops, SparseCore 0:
  9.4 46.1 all-gather.14
  57.3 37.7 all-gather.16
  96.8 43.5 all-gather.10
  142.0 55.4 all-gather.18
  199.0 52.9 all-gather.20
  253.6 52.9 all-gather.12
